TPU v7x, 128 devices: a whole 4x4x4 slice. The times are simulated.
128 devices in a mesh: row: 4 (over x_hi, core), col: 4 (over z), depth: 8 (over y, x_lo).
Axes of the slice: x: 4 (x_hi: 2, x_lo: 2; x = x_hi * 2 + x_lo), y: 4, z: 4, core: 2. Of those that a mesh axis runs over, the one named last changes fastest.
Arguments:
- a_blocks: bfloat16 [32, 4, 4, 16, 128, 128], P(None, 'col', 'row', 'depth'), may hold values from -6 to 6
- a_rows: int32 [32, 4, 4, 16], replicated, may hold values from -1 to 31, as said below
- b_blocks: bfloat16 [32, 4, 4, 8, 128, 128], P(None, 'row', 'col', 'depth'), may hold values from -0.15625 to 0.15625
- b_cols: int32 [32, 4, 4, 8], replicated, may hold values from -1 to 15, as said below
- c_pos: int32 [4, 4, 128], P('row', 'col'), may hold values from -1 to 511, as said below
Outputs:
- c_blocks: bfloat16 [4, 4, 128, 128, 128], P('row', 'col', 'depth')
Inputs may be any that keep to these rules, and one draw needn't show every extreme that they name: `a_rows`: for each inner block (g, m) and row group i the live slots come first and hold distinct local block rows, the rest hold -1; each has at least one live slot, and in every draw some (g, m, i) has all 16 slots live. `b_cols`: for each inner block (g, m) and column group h the live slots come first and hold distinct local block columns, the rest hold -1; each has at least one live slot, and in every draw some (g, m, h) has all 8 slots live. `c_pos`: each cell lists distinct positions in its first slots and -1 in the rest; every cell keeps at least one block, and in every draw some cell keeps 128.
All inputs are finite; a program needn't handle non-finite values.
Results may differ from a plain program's by a relative error of at most 0.001.
Values may be sent and summed in bfloat16 or wider, within the bound.
A program may use at most 320 MiB of HBM per device.

v0:
```python
import jax
import jax.numpy as jnp
from jax import lax
from jax.experimental import pallas as pl
from jax.experimental.pallas import tpu as pltpu
from jax.sharding import PartitionSpec as P

MESH = pl.DeviceIdType.MESH
BS = 128
NBL = 16
ANY = pl.BlockSpec(memory_space=pl.ANY)


def place():
    row, z, depth = lax.axis_index("row"), lax.axis_index("col"), lax.axis_index("depth")
    return row // 2, depth % 2, row % 2, depth // 2, z


def device(x_hi, x_lo, core, y, z):
    return (x_hi * 2 + core, z, y * 2 + x_lo)


def remote(src, dst, send, recv, to):
    return pltpu.make_async_remote_copy(
        src_ref=src, dst_ref=dst, send_sem=send, recv_sem=recv, device_id=to, device_id_type=MESH
    )


STEPS = (0, 1, 3, 2)
TOP = 32767.0
TINY = 2e-34
HALF = 8
ZERO = 32
NONE = ZERO * 64


def kernel(
    a_ref, b_ref, c_ref, rows_ref, cols_ref, out_ref,
    a00, a01, a02, a03, a10, a11, a12, a13, b0, b1, spots, codes, jobs, total, other, done, q_out, s_out, q_in, s_in,
    az_out, az_recv, az_ring, az_got, bx_out, bx_recv, bx_ring, bx_got, c_sem,
    twin_sem, q_send, q_recv, s_send, s_recv, out_sem,
):
    x_hi, x_lo, core, y, z = place()
    x = x_hi * 2 + x_lo
    same = x_lo == core
    apart = jnp.where(same, 0, 1)
    a_half, b_half = ((a00, a01, a02, a03), (a10, a11, a12, a13)), (b0, b1)

    def turned(at, step):
        return lax.rem(at + step + 8, 4)

    def differ(at, flag):
        return at if flag == 0 else 1 - at

    def z_to(step):
        return device(x_hi, x_lo, core, y, turned(z, step))

    def x_to(step):
        to = turned(x, step)
        return device(to // 2, lax.rem(to, 2), core, y, z)

    def y_to(step):
        return device(x_hi, x_lo, core, turned(y, step), z)

    twin = device(x_hi, x_lo, 1 - core, y, z)
    owner = device(x_hi, core, x_lo, y, z)

    barrier = pltpu.get_barrier_semaphore()

    def greet(to):
        pl.semaphore_signal(barrier, inc=1, device_id=to, device_id_type=MESH)

    for dy in STEPS:
        for flag in range(2):
            if (dy, flag) == (0, 0):

                @pl.when(jnp.logical_not(same))
                def _():
                    greet(twin)

            else:
                greet(device(x_hi, differ(x_lo, flag), x_lo, turned(y, -dy), z))
                greet(device(x_hi, x_lo, differ(core, flag), turned(y, -dy), z))
    for step in (1, -1):
        greet(z_to(step))
        greet(x_to(step))
    pl.semaphore_wait(barrier, 18 + apart)

    waits = []

    def send(src, dst, sent, recv, to):
        copy = remote(src, dst, sent, recv, to)
        copy.start()
        waits.append(copy.wait_send)

    def landed(piece, recv):
        remote(piece, piece, recv, recv, twin).wait_recv()

    def a_piece(half, back, at_y, at_lo):
        return a_half[half][back].at[pl.ds(at_y * 8 + at_lo * 4, 4)]

    def a_pieces(half, back, at_y):
        return a_half[half][back].at[pl.ds(at_y * 8, 8)]

    def b_piece(half, at_x, at_y, at_core):
        return b_half[half].at[pl.ds(at_x * 16 + at_y * 4 + at_core * 2, 2)]

    def b_pieces(half, at_x, at_y):
        return b_half[half].at[pl.ds(at_x * 16 + at_y * 4, 4)]

    def hand_out(half):
        for n, dy in enumerate(STEPS):
            for flag in range(2):
                to_y, to_core = turned(y, dy), differ(core, flag)
                group = (to_y * 2 + to_core) * 4 + half * 2
                src, dst = a_ref.at[pl.ds(group * 2, 4)], a_piece(half, 0, y, x_lo)
                sent, recv = az_out.at[half, n * 2 + flag], az_recv.at[half, n * 2 + apart]
                to = device(x_hi, core, to_core, to_y, z)
                if (dy, flag) == (0, 0):
                    hand_out_here(src, dst, sent, recv, to)
                else:
                    send(src, dst, sent, recv, to)
        for n, dy in enumerate(STEPS):
            for flag in range(2):
                to_y, to_core = turned(y, dy), differ(core, flag)
                group = (to_y * 2 + to_core) * 4 + half * 2
                src, dst = b_ref.at[pl.ds(group, 2)], b_piece(half, x, y, core)
                sent, recv = bx_out.at[half, n * 2 + flag], bx_recv.at[half, n * 2 + flag]
                if (dy, flag) == (0, 0):
                    pltpu.make_async_copy(src, dst, recv).start()
                else:
                    send(src, dst, sent, recv, device(x_hi, x_lo, to_core, to_y, z))

    def hand_out_here(src, dst, sent, recv, to):
        copy = remote(src, dst, sent, recv, to)
        stay = pltpu.make_async_copy(src, dst, recv)
        pl.when(same)(lambda: stay.start())
        pl.when(jnp.logical_not(same))(lambda: copy.start())
        waits.append(lambda: pl.when(jnp.logical_not(same))(lambda: copy.wait_send()))

    def turn_a(half, n):
        at = turned(y, -STEPS[n])
        for flag in range(2):
            landed(a_piece(half, 0, at, differ(x_lo, flag)), az_recv.at[half, n * 2 + flag])
        for back, step in ((1, 1), (3, -1)):
            send(
                a_pieces(half, 0, at), a_pieces(half, back, at), az_ring.at[half, back, n],
                az_got.at[half, back, n], z_to(step),
            )

    def pass_a(half, n):
        at = turned(y, -STEPS[n])
        back, step = (1, 1) if n % 2 == 0 else (3, -1)
        landed(a_pieces(half, back, at), az_got.at[half, back, n])
        send(
            a_pieces(half, back, at), a_pieces(half, 2, at), az_ring.at[half, 2, n], az_got.at[half, 2, n],
            z_to(step),
        )

    def rest_a(half, back):
        for n in range(4):
            if back == 2 or back != (1 if n % 2 == 0 else 3):
                landed(a_pieces(half, back, turned(y, -STEPS[n])), az_got.at[half, back, n])

    def turn_b(half, n):
        at = turned(y, -STEPS[n])
        for flag in range(2):
            landed(b_piece(half, x, at, differ(core, flag)), bx_recv.at[half, n * 2 + flag])
        here = b_pieces(half, x, at)
        for back, step in ((1, 1), (3, -1)):
            send(here, here, bx_ring.at[half, back, n], bx_got.at[half, back, n], x_to(step))

    def pass_b(half, n):
        back, step = (1, 1) if n % 2 == 0 else (3, -1)
        there = b_pieces(half, turned(x, -back), turned(y, -STEPS[n]))
        landed(there, bx_got.at[half, back, n])
        send(there, there, bx_ring.at[half, 2, n], bx_got.at[half, 2, n], x_to(step))

    def rest_b(half):
        for n in range(4):
            for back in (3 if n % 2 == 0 else 1, 2):
                landed(b_pieces(half, turned(x, -back), turned(y, -STEPS[n])), bx_got.at[half, back, n])

    def pair_up():
        landed(spots.at[1], c_sem.at[1])
        spot = jnp.where(same, c_ref[0], spots[1, 0])
        kept_row = jnp.where(spot >= 0, spot // NBL, -2)
        kept_col = jnp.where(spot >= 0, spot % NBL, -2)
        k = lax.broadcasted_iota(jnp.int32, (16, BS), 0)
        group, m = (k // 4) % 2, k % 4
        a_at = jnp.full((16, BS), -1, jnp.int32)
        b_at = jnp.full((16, BS), -1, jnp.int32)
        row_values, col_values = rows_ref[...], cols_ref[...]
        for u in range(16):
            a_at = jnp.where(row_values[:, u : u + 1] == kept_row, group * 2 + (u // 2 * 4 + u % 2), a_at)
        b_base = (m // 2) * 32 + (m % 2) * 2 + group
        for v in range(8):
            b_at = jnp.where(col_values[:, v : v + 1] == kept_col, b_base + (v % 2 * 16 + v // 2 * 4), b_at)
        codes[...] = jnp.where((a_at >= 0) & (b_at >= 0), a_at * 64 + b_at, NONE)
        copy = pltpu.make_async_copy(codes, jobs, c_sem.at[2])
        copy.start()
        copy.wait()

    def add_products(half, back, first, count, fresh=False):
        left_ref, right_ref = a_half[half][back], b_half[half]
        k = half * 8 + turned(z, -back)

        def some(n, _):
            for s in range(32):
                slot = first + n * 32 + s
                one, two = jobs[k, slot], jobs[k + 4, slot]
                left = jnp.concatenate([left_ref[one >> 6], left_ref[two >> 6]], axis=1)
                right = jnp.concatenate([right_ref[one & 63], right_ref[two & 63]], axis=0)
                term = jnp.dot(left, right, preferred_element_type=jnp.float32)
                if fresh:
                    total[slot] = term
                else:
                    total[slot] += term
            return 0

        lax.fori_loop(0, count // 32, some, 0)

    hand_out(0)
    send(c_ref, spots.at[1], c_sem.at[0], c_sem.at[1], twin)
    for half in a_half:
        for ref in half:
            ref[ZERO] = jnp.zeros((BS, BS), jnp.bfloat16)
    turn_a(0, 0)
    turn_b(0, 0)
    turn_a(0, 1)
    pass_a(0, 0)
    turn_a(0, 2)
    pass_a(0, 1)
    turn_a(0, 3)
    turn_b(0, 1)
    turn_b(0, 2)
    hand_out(1)
    turn_b(0, 3)
    pass_a(0, 2)
    pass_b(0, 0)
    pass_b(0, 1)
    pass_a(0, 3)
    pass_b(0, 2)
    pass_b(0, 3)
    pair_up()
    for n in range(4):
        turn_a(1, n)
    turn_b(1, 0)
    turn_b(1, 1)
    rest_b(0)
    add_products(0, 0, 0, BS, fresh=True)
    turn_b(1, 2)
    turn_b(1, 3)
    rest_a(0, 1)
    add_products(0, 1, 0, BS)
    pass_a(1, 0)
    pass_b(1, 0)
    pass_b(1, 1)
    rest_a(0, 3)
    add_products(0, 3, 0, BS)
    pass_a(1, 1)
    pass_b(1, 2)
    pass_b(1, 3)
    rest_a(0, 2)
    add_products(0, 2, 0, BS)
    pass_a(1, 2)
    rest_b(1)
    add_products(1, 0, 0, BS)
    pass_a(1, 3)
    rest_a(1, 1)
    add_products(1, 1, 0, BS)
    rest_a(1, 3)
    add_products(1, 3, 0, BS)
    rest_a(1, 2)

    def start_of(r):
        return turned(y, r) * 32

    for r in (2, 1, 3, 0):
        add_products(1, 2, start_of(r), 32)
        send(
            total.at[pl.ds(start_of(r) + (1 - core) * 16, 16)], other.at[r], twin_sem.at[0, r],
            twin_sem.at[1, r], twin,
        )

    def meet(r):
        landed(other.at[r], twin_sem.at[1, r])

    def arrived(i):
        landed(q_in.at[i], q_recv.at[i])
        landed(s_in.at[i], s_recv.at[i])

    def chip_sum(r, slot):
        return total[start_of(r) + core * 16 + slot] + other[r, slot]

    def value(i, n):
        return q_in[i, n].astype(jnp.float32) * s_in[i, pl.ds(n, 1)]

    def tell(i, step, r, first, plus=None):
        def one(n, _):
            sums = chip_sum(r, first + n)
            if plus is not None:
                sums = sums + value(plus, n)
            top = jnp.maximum(jnp.max(jnp.abs(sums), axis=0, keepdims=True), TINY)
            q_out[i, n] = jnp.round(sums * (TOP / top)).astype(jnp.int32).astype(jnp.int16)
            s_out[i, pl.ds(n, 1)] = top * (1 / TOP)
            return 0

        lax.fori_loop(0, HALF, one, 0)
        send(q_out.at[i], q_in.at[i], q_send.at[i], q_recv.at[i], y_to(step))
        send(s_out.at[i], s_in.at[i], s_send.at[i], s_recv.at[i], y_to(step))

    meet(2)
    tell(0, 1, 2, 0)
    tell(1, -1, 2, HALF)
    meet(1)
    tell(2, 1, 1, HALF)
    meet(3)
    tell(3, -1, 3, 0)
    arrived(0)
    tell(4, 1, 1, 0, plus=0)
    arrived(1)
    tell(5, -1, 3, HALF, plus=1)
    meet(0)

    def finish(half, first, second):
        def one(n, _):
            slot = half * HALF + n
            sums = chip_sum(0, slot) + value(first, n) + value(second, n)
            done[slot] = sums.astype(jnp.bfloat16)
            return 0

        lax.fori_loop(0, HALF, one, 0)
        span = pl.ds(half * HALF, HALF)
        hand_out_here(done.at[span], out_ref.at[span], out_sem.at[0, half], out_sem.at[1, half], owner)

    arrived(3)
    arrived(4)
    finish(0, 3, 4)
    arrived(2)
    arrived(5)
    finish(1, 2, 5)
    for half in range(2):
        landed(out_ref.at[pl.ds(half * HALF, HALF)], out_sem.at[1, half])
    for wait in waits:
        wait()


def per_device(a_blocks, a_rows, b_blocks, b_cols, c_pos):
    x_hi, x_lo, core, y, z = place()
    layer = y * 2 + core
    rows = lax.dynamic_slice(a_rows, (layer * 4, 0, x_hi * 2 + x_lo, 0), (4, 4, 1, 16)).reshape(16, 16)
    cols = lax.dynamic_slice(b_cols, (layer * 4, 0, z, 0), (4, 4, 1, 8)).reshape(16, 8)
    dma = pltpu.SemaphoreType.DMA
    vmem = pl.BlockSpec(memory_space=pltpu.VMEM)
    bf16, f32, i16, i32 = jnp.bfloat16, jnp.float32, jnp.int16, jnp.int32
    out = pl.pallas_call(
        kernel,
        out_shape=jax.ShapeDtypeStruct((16, BS, BS), bf16),
        in_specs=[ANY, ANY, vmem, vmem, vmem],
        out_specs=vmem,
        scratch_shapes=[
            *[pltpu.VMEM((ZERO + 1, BS, BS), bf16)] * 8,
            *[pltpu.VMEM((64, BS, BS), bf16)] * 2,
            pltpu.VMEM((2,) + c_pos.shape, i32),
            pltpu.VMEM((16, BS), i32),
            pltpu.SMEM((16, BS), i32),
            pltpu.VMEM((BS, BS, BS), f32),
            pltpu.VMEM((4, 16, BS, BS), f32),
            pltpu.VMEM((16, BS, BS), bf16),
            pltpu.VMEM((6, HALF, BS, BS), i16),
            pltpu.VMEM((6, HALF, BS), f32),
            pltpu.VMEM((6, HALF, BS, BS), i16),
            pltpu.VMEM((6, HALF, BS), f32),
            dma((2, 8)), dma((2, 8)), dma((2, 4, 4)), dma((2, 4, 4)),
            dma((2, 8)), dma((2, 8)), dma((2, 4, 4)), dma((2, 4, 4)), dma((3,)),
            dma((2, 4)), dma((6,)), dma((6,)), dma((6,)), dma((6,)), dma((2, 2)),
        ],
        compiler_params=pltpu.CompilerParams(
            collective_id=0, has_side_effects=True, vmem_limit_bytes=60 * 2**20
        ),
        name="block_product",
    )(a_blocks.reshape(64, BS, BS), b_blocks.reshape(32, BS, BS), c_pos, rows, cols)
    return out[None, None]


def solution(mesh):
    placed = (
        P(None, "col", "row", "depth", None, None),
        P(),
        P(None, "row", "col", "depth", None, None),
        P(),
        P("row", "col", None),
    )
    return jax.shard_map(
        per_device,
        mesh=mesh,
        in_specs=placed,
        out_specs=P("row", "col", "depth", None, None),
        check_vma=False,
    )
```

profile of v0, /device:TPU:1, one launch (start us, length us, event | category | flops | bytes accessed | tf_op | source)
XLA Modules:
  0.0 120.1 jit_solution(6548620908045744082)
XLA Ops:
  0.0 0.0 copy-start
  0.0 0.8 constant_dynamic-slice_fusion
  0.8 0.7 copy.7
  1.5 0.0 copy-done
  1.5 0.1 constant_dynamic-slice_fusion.1
  1.6 0.7 copy.6
  2.3 115.9 %block_product.1 = bf16[16,128,128]{2,1,0:T(8,128)(2,1)} custom-call(bf16[64,128,128]{2,1,0:T(8,128)(2,1)} %bitcast.5, bf16[32,128,128]{2,1,0:T(8,128)(2,1)} %bitcast.7, s32[1,1,128]{2,1,0:T(1,128)} %c_ref.1, s32[16,16]{1,0:T(8,128)} %bitcast.9, s32[16,8]{1,0:T(8,128)} %bitcast.8), custom_call_target="tpu_custom_call" | custom-call | tf_op jit(solution)/shard_map/block_product/pallas_call | solution.py:357
  118.2 1.9 %copy.9 = bf16[1,1,16,128,128]{4,3,2,1,0:T(8,128)(2,1)} copy(bf16[1,1,16,128,128]{4,3,2,1,0:T(8,128)(2,1)} %bitcast.6) | data formatting | bytes 1048576
Async XLA Ops:
  0.0 1.5 %copy-start = (s32[32,4,4,16]{0,3,2,1:T(8,128)S(1)}, s32[32,4,4,16]{0,3,2,1:T(8,128)}, u32[]{:S(2)}) copy-start(s32[32,4,4,16]{0,3,2,1:T(8,128)} %param.6) | copy-start | bytes 98308
where the time goes:
time: 120 us
  Pallas kernels  116 us (97%)
  local copies, waits for them, and re-layouts  4.17 us (3%)
    pallas_call x1, Pallas kernels, per_device(): pl.pallas_call(kernel, out_shape=jax.ShapeDtypeStruct((16, BS, BS), bf16)...  116 us

commit v1 on v0

--- a/solution.py
+++ b/solution.py
@@ -27,16 +27,17 @@
 
 
 STEPS = (0, 1, 3, 2)
+UNITS = ((0, 0), (0, 1), (1, None), (2, None), (3, 0), (3, 1))
 TOP = 32767.0
 TINY = 2e-34
-HALF = 8
+PART = 4
 ZERO = 32
 NONE = ZERO * 64
 
 
 def kernel(
     a_ref, b_ref, c_ref, rows_ref, cols_ref, out_ref,
-    a00, a01, a02, a03, a10, a11, a12, a13, b0, b1, spots, codes, jobs, total, other, done, q_out, s_out, q_in, s_in,
+    a00, a01, a02, a03, a10, a11, a12, a13, b0, b1, spots, rows, cols, codes, jobs, total, other, done, q_out, s_out, q_in, s_in,
     az_out, az_recv, az_ring, az_got, bx_out, bx_recv, bx_ring, bx_got, c_sem,
     twin_sem, q_send, q_recv, s_send, s_recv, out_sem,
 ):
@@ -138,29 +139,33 @@
         pl.when(jnp.logical_not(same))(lambda: copy.start())
         waits.append(lambda: pl.when(jnp.logical_not(same))(lambda: copy.wait_send()))
 
-    def turn_a(half, n):
+    def a_unit(half, back, i):
+        n, flag = UNITS[i]
         at = turned(y, -STEPS[n])
-        for flag in range(2):
-            landed(a_piece(half, 0, at, differ(x_lo, flag)), az_recv.at[half, n * 2 + flag])
+        return a_pieces(half, back, at) if flag is None else a_piece(half, back, at, differ(x_lo, flag))
+
+    def turn_a(half, i):
+        n, flag = UNITS[i]
+        for one in range(2) if flag is None else (flag,):
+            piece = a_piece(half, 0, turned(y, -STEPS[n]), differ(x_lo, one))
+            landed(piece, az_recv.at[half, n * 2 + one])
         for back, step in ((1, 1), (3, -1)):
             send(
-                a_pieces(half, 0, at), a_pieces(half, back, at), az_ring.at[half, back, n],
-                az_got.at[half, back, n], z_to(step),
+                a_unit(half, 0, i), a_unit(half, back, i), az_ring.at[half, back, i], az_got.at[half, back, i],
+                z_to(step),
             )
 
-    def pass_a(half, n):
-        at = turned(y, -STEPS[n])
-        back, step = (1, 1) if n % 2 == 0 else (3, -1)
-        landed(a_pieces(half, back, at), az_got.at[half, back, n])
+    def pass_a(half, i):
+        back, step = (1, 1) if i % 2 == 0 else (3, -1)
+        landed(a_unit(half, back, i), az_got.at[half, back, i])
         send(
-            a_pieces(half, back, at), a_pieces(half, 2, at), az_ring.at[half, 2, n], az_got.at[half, 2, n],
-            z_to(step),
+            a_unit(half, back, i), a_unit(half, 2, i), az_ring.at[half, 2, i], az_got.at[half, 2, i], z_to(step)
         )
 
     def rest_a(half, back):
-        for n in range(4):
-            if back == 2 or back != (1 if n % 2 == 0 else 3):
-                landed(a_pieces(half, back, turned(y, -STEPS[n])), az_got.at[half, back, n])
+        for i in range(len(UNITS)):
+            if back == 2 or back != (1 if i % 2 == 0 else 3):
+                landed(a_unit(half, back, i), az_got.at[half, back, i])
 
     def turn_b(half, n):
         at = turned(y, -STEPS[n])
@@ -182,21 +187,32 @@
                 landed(b_pieces(half, turned(x, -back), turned(y, -STEPS[n])), bx_got.at[half, back, n])
 
     def pair_up():
+        for copy in index_copies:
+            copy.wait()
         landed(spots.at[1], c_sem.at[1])
-        spot = jnp.where(same, c_ref[0], spots[1, 0])
+        spot = jnp.where(same, spots[0, 0], spots[1, 0])
         kept_row = jnp.where(spot >= 0, spot // NBL, -2)
         kept_col = jnp.where(spot >= 0, spot % NBL, -2)
-        k = lax.broadcasted_iota(jnp.int32, (16, BS), 0)
-        group, m = (k // 4) % 2, k % 4
-        a_at = jnp.full((16, BS), -1, jnp.int32)
-        b_at = jnp.full((16, BS), -1, jnp.int32)
-        row_values, col_values = rows_ref[...], cols_ref[...]
-        for u in range(16):
-            a_at = jnp.where(row_values[:, u : u + 1] == kept_row, group * 2 + (u // 2 * 4 + u % 2), a_at)
-        b_base = (m // 2) * 32 + (m % 2) * 2 + group
-        for v in range(8):
-            b_at = jnp.where(col_values[:, v : v + 1] == kept_col, b_base + (v % 2 * 16 + v // 2 * 4), b_at)
-        codes[...] = jnp.where((a_at >= 0) & (b_at >= 0), a_at * 64 + b_at, NONE)
+
+        def number_of(index, kept, number):
+            slots, groups = index.shape
+
+            def one(g):
+                lane = lax.broadcasted_iota(jnp.int32, (slots, groups), 1)
+                mine = jnp.sum(jnp.where(lane == g, index, 0), axis=1, keepdims=True)
+                return jnp.max(jnp.where(mine == kept, number, -1), axis=0, keepdims=True)
+
+            return one
+
+        u = lax.broadcasted_iota(jnp.int32, (16, BS), 0)
+        v = lax.broadcasted_iota(jnp.int32, (8, BS), 0)
+        for m in range(4):
+            row_of = number_of(rows[m], kept_row, (u >> 1) * 4 + (u & 1))
+            col_of = number_of(cols[m], kept_col, (v & 1) * 16 + (v >> 1) * 4)
+            for n in range(4):
+                a_at, b_at = row_of((y * 2 + core) * 4 + n), col_of((y * 2 + core) * 4 + n)
+                code = (a_at + n % 2 * 2) * 64 + b_at + (m // 2 * 32 + m % 2 * 2 + n % 2)
+                codes[n * 4 + m : n * 4 + m + 1] = jnp.where((a_at >= 0) & (b_at >= 0), code, NONE)
         copy = pltpu.make_async_copy(codes, jobs, c_sem.at[2])
         copy.start()
         copy.wait()
@@ -222,29 +238,44 @@
 
     hand_out(0)
     send(c_ref, spots.at[1], c_sem.at[0], c_sem.at[1], twin)
+    index_copies = [
+        pltpu.make_async_copy(c_ref, spots.at[0], c_sem.at[2]),
+        pltpu.make_async_copy(rows_ref.at[:, x], rows, c_sem.at[3]),
+        pltpu.make_async_copy(cols_ref.at[:, z], cols, c_sem.at[4]),
+    ]
+    for copy in index_copies:
+        copy.start()
     for half in a_half:
         for ref in half:
             ref[ZERO] = jnp.zeros((BS, BS), jnp.bfloat16)
     turn_a(0, 0)
+    turn_a(0, 1)
     turn_b(0, 0)
-    turn_a(0, 1)
+    turn_a(0, 2)
     pass_a(0, 0)
-    turn_a(0, 2)
     pass_a(0, 1)
     turn_a(0, 3)
+    pass_a(0, 2)
+    turn_a(0, 4)
+    turn_a(0, 5)
     turn_b(0, 1)
     turn_b(0, 2)
     hand_out(1)
     turn_b(0, 3)
-    pass_a(0, 2)
+    pass_a(0, 3)
     pass_b(0, 0)
     pass_b(0, 1)
-    pass_a(0, 3)
+    pass_a(0, 4)
+    pass_a(0, 5)
     pass_b(0, 2)
     pass_b(0, 3)
     pair_up()
-    for n in range(4):
-        turn_a(1, n)
+    turn_a(1, 0)
+    turn_a(1, 1)
+    turn_a(1, 2)
+    turn_a(1, 3)
+    turn_a(1, 4)
+    turn_a(1, 5)
     turn_b(1, 0)
     turn_b(1, 1)
     rest_b(0)
@@ -254,19 +285,21 @@
     rest_a(0, 1)
     add_products(0, 1, 0, BS)
     pass_a(1, 0)
+    pass_a(1, 1)
     pass_b(1, 0)
     pass_b(1, 1)
     rest_a(0, 3)
     add_products(0, 3, 0, BS)
-    pass_a(1, 1)
+    pass_a(1, 2)
     pass_b(1, 2)
     pass_b(1, 3)
     rest_a(0, 2)
     add_products(0, 2, 0, BS)
-    pass_a(1, 2)
+    pass_a(1, 3)
     rest_b(1)
     add_products(1, 0, 0, BS)
-    pass_a(1, 3)
+    pass_a(1, 4)
+    pass_a(1, 5)
     rest_a(1, 1)
     add_products(1, 1, 0, BS)
     rest_a(1, 3)
@@ -276,15 +309,17 @@
     def start_of(r):
         return turned(y, r) * 32
 
-    for r in (2, 1, 3, 0):
+    def end_products(r):
         add_products(1, 2, start_of(r), 32)
-        send(
-            total.at[pl.ds(start_of(r) + (1 - core) * 16, 16)], other.at[r], twin_sem.at[0, r],
-            twin_sem.at[1, r], twin,
-        )
-
-    def meet(r):
-        landed(other.at[r], twin_sem.at[1, r])
+        for part in range(4):
+            span = pl.ds(part * PART, PART)
+            send(
+                total.at[pl.ds(start_of(r) + (1 - core) * 16 + part * PART, PART)], other.at[r, span],
+                twin_sem.at[0, r, part], twin_sem.at[1, r, part], twin,
+            )
+
+    def meet(r, part):
+        landed(other.at[r, pl.ds(part * PART, PART)], twin_sem.at[1, r, part])
 
     def arrived(i):
         landed(q_in.at[i], q_recv.at[i])
@@ -297,6 +332,8 @@
         return q_in[i, n].astype(jnp.float32) * s_in[i, pl.ds(n, 1)]
 
     def tell(i, step, r, first, plus=None):
+        meet(r, first // PART)
+
         def one(n, _):
             sums = chip_sum(r, first + n)
             if plus is not None:
@@ -306,75 +343,80 @@
             s_out[i, pl.ds(n, 1)] = top * (1 / TOP)
             return 0
 
-        lax.fori_loop(0, HALF, one, 0)
+        lax.fori_loop(0, PART, one, 0)
         send(q_out.at[i], q_in.at[i], q_send.at[i], q_recv.at[i], y_to(step))
         send(s_out.at[i], s_in.at[i], s_send.at[i], s_recv.at[i], y_to(step))
 
-    meet(2)
-    tell(0, 1, 2, 0)
-    tell(1, -1, 2, HALF)
-    meet(1)
-    tell(2, 1, 1, HALF)
-    meet(3)
-    tell(3, -1, 3, 0)
-    arrived(0)
-    tell(4, 1, 1, 0, plus=0)
-    arrived(1)
-    tell(5, -1, 3, HALF, plus=1)
-    meet(0)
-
-    def finish(half, first, second):
+    end_products(2)
+    for part in range(2):
+        tell(part, 1, 2, part * PART)
+        tell(2 + part, -1, 2, (2 + part) * PART)
+    end_products(1)
+    end_products(3)
+    for part in range(2):
+        tell(4 + part, 1, 1, (2 + part) * PART)
+    end_products(0)
+    for part in range(2):
+        tell(6 + part, -1, 3, part * PART)
+    for part in range(2):
+        arrived(part)
+        tell(8 + part, 1, 1, part * PART, plus=part)
+        arrived(2 + part)
+        tell(10 + part, -1, 3, (2 + part) * PART, plus=2 + part)
+
+    def finish(part, first, second):
+        meet(0, part)
+        arrived(first)
+        arrived(second)
+
         def one(n, _):
-            slot = half * HALF + n
+            slot = part * PART + n
             sums = chip_sum(0, slot) + value(first, n) + value(second, n)
             done[slot] = sums.astype(jnp.bfloat16)
             return 0
 
-        lax.fori_loop(0, HALF, one, 0)
-        span = pl.ds(half * HALF, HALF)
-        hand_out_here(done.at[span], out_ref.at[span], out_sem.at[0, half], out_sem.at[1, half], owner)
-
-    arrived(3)
-    arrived(4)
-    finish(0, 3, 4)
-    arrived(2)
-    arrived(5)
-    finish(1, 2, 5)
-    for half in range(2):
-        landed(out_ref.at[pl.ds(half * HALF, HALF)], out_sem.at[1, half])
+        lax.fori_loop(0, PART, one, 0)
+        span = pl.ds(part * PART, PART)
+        hand_out_here(done.at[span], out_ref.at[span], out_sem.at[0, part], out_sem.at[1, part], owner)
+
+    finish(0, 6, 8)
+    finish(2, 4, 10)
+    finish(1, 7, 9)
+    finish(3, 5, 11)
+    for part in range(4):
+        landed(out_ref.at[pl.ds(part * PART, PART)], out_sem.at[1, part])
     for wait in waits:
         wait()
 
 
 def per_device(a_blocks, a_rows, b_blocks, b_cols, c_pos):
-    x_hi, x_lo, core, y, z = place()
-    layer = y * 2 + core
-    rows = lax.dynamic_slice(a_rows, (layer * 4, 0, x_hi * 2 + x_lo, 0), (4, 4, 1, 16)).reshape(16, 16)
-    cols = lax.dynamic_slice(b_cols, (layer * 4, 0, z, 0), (4, 4, 1, 8)).reshape(16, 8)
+    rows, cols = a_rows.transpose(1, 2, 3, 0), b_cols.transpose(1, 2, 3, 0)
     dma = pltpu.SemaphoreType.DMA
     vmem = pl.BlockSpec(memory_space=pltpu.VMEM)
     bf16, f32, i16, i32 = jnp.bfloat16, jnp.float32, jnp.int16, jnp.int32
     out = pl.pallas_call(
         kernel,
         out_shape=jax.ShapeDtypeStruct((16, BS, BS), bf16),
-        in_specs=[ANY, ANY, vmem, vmem, vmem],
+        in_specs=[ANY] * 5,
         out_specs=vmem,
         scratch_shapes=[
             *[pltpu.VMEM((ZERO + 1, BS, BS), bf16)] * 8,
             *[pltpu.VMEM((64, BS, BS), bf16)] * 2,
             pltpu.VMEM((2,) + c_pos.shape, i32),
+            pltpu.VMEM((4, 16, 32), i32),
+            pltpu.VMEM((4, 8, 32), i32),
             pltpu.VMEM((16, BS), i32),
             pltpu.SMEM((16, BS), i32),
             pltpu.VMEM((BS, BS, BS), f32),
             pltpu.VMEM((4, 16, BS, BS), f32),
             pltpu.VMEM((16, BS, BS), bf16),
-            pltpu.VMEM((6, HALF, BS, BS), i16),
-            pltpu.VMEM((6, HALF, BS), f32),
-            pltpu.VMEM((6, HALF, BS, BS), i16),
-            pltpu.VMEM((6, HALF, BS), f32),
-            dma((2, 8)), dma((2, 8)), dma((2, 4, 4)), dma((2, 4, 4)),
-            dma((2, 8)), dma((2, 8)), dma((2, 4, 4)), dma((2, 4, 4)), dma((3,)),
-            dma((2, 4)), dma((6,)), dma((6,)), dma((6,)), dma((6,)), dma((2, 2)),
+            pltpu.VMEM((12, PART, BS, BS), i16),
+            pltpu.VMEM((12, PART, BS), f32),
+            pltpu.VMEM((12, PART, BS, BS), i16),
+            pltpu.VMEM((12, PART, BS), f32),
+            dma((2, 8)), dma((2, 8)), dma((2, 4, 6)), dma((2, 4, 6)),
+            dma((2, 8)), dma((2, 8)), dma((2, 4, 4)), dma((2, 4, 4)), dma((5,)),
+            dma((2, 4, 4)), dma((12,)), dma((12,)), dma((12,)), dma((12,)), dma((2, 4)),
         ],
         compiler_params=pltpu.CompilerParams(
             collective_id=0, has_side_effects=True, vmem_limit_bytes=60 * 2**20

time: 120 us -> 111 us (0.925)
  Pallas kernels: 116 us -> 109 us
  local copies, waits for them, and re-layouts: 4.17 us -> 1.89 us
    pallas_call x1, Pallas kernels: 116 us -> 109 us  [per_device(): pl.pallas_call(kernel, out_shape=jax.ShapeDtypeStruct((16, BS, BS), bf16)...]
    dynamic_slice x4 -> x0, local copies, waits for them, and re-layouts: 2.28 us -> none  [the longest x2 1.51 us: per_device(): lax.dynamic_slice(b_cols, (layer * 4, 0, z, 0), (4, 4, 1, 8)).reshape(16, 8)]
where the time goes in v1:
time: 111 us
  Pallas kernels  109 us (98%)
  local copies, waits for them, and re-layouts  1.89 us (2%)
    pallas_call x1, Pallas kernels, per_device(): pl.pallas_call(kernel, out_shape=jax.ShapeDtypeStruct((16, BS, BS), bf16)...  109 us

profile of v1, /device:TPU:1, one launch (start us, length us, event | category | flops | bytes accessed | tf_op | source)
XLA Modules:
  0.0 110.7 jit_solution(5505431681571214750)
XLA Ops:
  0.0 108.8 %block_product.1 = bf16[16,128,128]{2,1,0:T(8,128)(2,1)} custom-call(bf16[64,128,128]{2,1,0:T(8,128)(2,1)} %bitcast.5, bf16[32,128,128]{2,1,0:T(8,128)(2,1)} %bitcast.7, s32[1,1,128]{2,1,0:T(1,128)} %c_ref.1, s32[4,4,16,32]{3,2,1,0:T(8,128)} %bitcast.8, s32[4,4,8,32]{3,2,1,0:T(8,128)} %bitcast.9), custom_call_target="tpu_custom_call" | custom-call | tf_op jit(solution)/shard_map/block_product/pallas_call | solution.py:397
  108.8 1.9 %copy.7 = bf16[1,1,16,128,128]{4,3,2,1,0:T(8,128)(2,1)} copy(bf16[1,1,16,128,128]{4,3,2,1,0:T(8,128)(2,1)} %bitcast.6) | data formatting | bytes 1048576

commit v2 on v1

--- a/solution.py
+++ b/solution.py
@@ -31,6 +31,7 @@
 TOP = 32767.0
 TINY = 2e-34
 PART = 4
+PARTS = 8 // PART
 ZERO = 32
 NONE = ZERO * 64
 
@@ -94,6 +95,10 @@
         copy.start()
         waits.append(copy.wait_send)
 
+    def settle(count):
+        for _ in range(count):
+            waits.pop(0)()
+
     def landed(piece, recv):
         remote(piece, piece, recv, recv, twin).wait_recv()
 
@@ -109,7 +114,7 @@
     def b_pieces(half, at_x, at_y):
         return b_half[half].at[pl.ds(at_x * 16 + at_y * 4, 4)]
 
-    def hand_out(half):
+    def hand_out_a(half):
         for n, dy in enumerate(STEPS):
             for flag in range(2):
                 to_y, to_core = turned(y, dy), differ(core, flag)
@@ -121,6 +126,8 @@
                     hand_out_here(src, dst, sent, recv, to)
                 else:
                     send(src, dst, sent, recv, to)
+
+    def hand_out_b(half):
         for n, dy in enumerate(STEPS):
             for flag in range(2):
                 to_y, to_core = turned(y, dy), differ(core, flag)
@@ -236,7 +243,9 @@
 
         lax.fori_loop(0, count // 32, some, 0)
 
-    hand_out(0)
+    hand_out_a(0)
+    turn_a(0, 0)
+    hand_out_b(0)
     send(c_ref, spots.at[1], c_sem.at[0], c_sem.at[1], twin)
     index_copies = [
         pltpu.make_async_copy(c_ref, spots.at[0], c_sem.at[2]),
@@ -248,7 +257,6 @@
     for half in a_half:
         for ref in half:
             ref[ZERO] = jnp.zeros((BS, BS), jnp.bfloat16)
-    turn_a(0, 0)
     turn_a(0, 1)
     turn_b(0, 0)
     turn_a(0, 2)
@@ -260,7 +268,8 @@
     turn_a(0, 5)
     turn_b(0, 1)
     turn_b(0, 2)
-    hand_out(1)
+    hand_out_a(1)
+    hand_out_b(1)
     turn_b(0, 3)
     pass_a(0, 3)
     pass_b(0, 0)
@@ -334,35 +343,42 @@
     def tell(i, step, r, first, plus=None):
         meet(r, first // PART)
 
-        def one(n, _):
+        def term(n):
             sums = chip_sum(r, first + n)
-            if plus is not None:
-                sums = sums + value(plus, n)
-            top = jnp.maximum(jnp.max(jnp.abs(sums), axis=0, keepdims=True), TINY)
-            q_out[i, n] = jnp.round(sums * (TOP / top)).astype(jnp.int32).astype(jnp.int16)
-            s_out[i, pl.ds(n, 1)] = top * (1 / TOP)
-            return 0
-
-        lax.fori_loop(0, PART, one, 0)
+            return sums if plus is None else sums + value(plus, n)
+
+        tops = [
+            jnp.maximum(jnp.max(jnp.abs(term(n)), axis=0, keepdims=True), TINY) for n in range(PART)
+        ]
+        for n, top in enumerate(tops):
+            s_out[i, n : n + 1] = top * (1 / TOP)
+        scales = [TOP / top for top in tops]
+        for n, scale in enumerate(scales):
+            q_out[i, n] = jnp.round(term(n) * scale).astype(jnp.int32).astype(jnp.int16)
         send(q_out.at[i], q_in.at[i], q_send.at[i], q_recv.at[i], y_to(step))
         send(s_out.at[i], s_in.at[i], s_send.at[i], s_recv.at[i], y_to(step))
 
+    gathered = len(waits)
     end_products(2)
-    for part in range(2):
+    for part in range(PARTS):
         tell(part, 1, 2, part * PART)
-        tell(2 + part, -1, 2, (2 + part) * PART)
+        tell(PARTS + part, -1, 2, 8 + part * PART)
     end_products(1)
+    for part in range(PARTS):
+        tell(2 * PARTS + part, 1, 1, 8 + part * PART)
     end_products(3)
-    for part in range(2):
-        tell(4 + part, 1, 1, (2 + part) * PART)
+    for part in range(PARTS // 2):
+        tell(3 * PARTS + part, -1, 3, part * PART)
     end_products(0)
-    for part in range(2):
-        tell(6 + part, -1, 3, part * PART)
-    for part in range(2):
+    settle(gathered)
+    handed = len(waits)
+    for part in range(PARTS):
+        arrived(PARTS + part)
+        tell(5 * PARTS + part, -1, 3, 8 + part * PART, plus=PARTS + part)
         arrived(part)
-        tell(8 + part, 1, 1, part * PART, plus=part)
-        arrived(2 + part)
-        tell(10 + part, -1, 3, (2 + part) * PART, plus=2 + part)
+        tell(4 * PARTS + part, 1, 1, part * PART, plus=part)
+    for part in range(PARTS // 2, PARTS):
+        tell(3 * PARTS + part, -1, 3, part * PART)
 
     def finish(part, first, second):
         meet(0, part)
@@ -379,14 +395,13 @@
         span = pl.ds(part * PART, PART)
         hand_out_here(done.at[span], out_ref.at[span], out_sem.at[0, part], out_sem.at[1, part], owner)
 
-    finish(0, 6, 8)
-    finish(2, 4, 10)
-    finish(1, 7, 9)
-    finish(3, 5, 11)
-    for part in range(4):
+    settle(handed)
+    for part in range(PARTS):
+        finish(PARTS + part, 2 * PARTS + part, 5 * PARTS + part)
+        finish(part, 3 * PARTS + part, 4 * PARTS + part)
+    for part in range(2 * PARTS):
         landed(out_ref.at[pl.ds(part * PART, PART)], out_sem.at[1, part])
-    for wait in waits:
-        wait()
+    settle(len(waits))
 
 
 def per_device(a_blocks, a_rows, b_blocks, b_cols, c_pos):
@@ -397,7 +412,7 @@
     out = pl.pallas_call(
         kernel,
         out_shape=jax.ShapeDtypeStruct((16, BS, BS), bf16),
-        in_specs=[ANY] * 5,
+        in_specs=[pl.BlockSpec(memory_space=pltpu.HBM)] * 5,
         out_specs=vmem,
         scratch_shapes=[
             *[pltpu.VMEM((ZERO + 1, BS, BS), bf16)] * 8,
@@ -410,19 +425,19 @@
             pltpu.VMEM((BS, BS, BS), f32),
             pltpu.VMEM((4, 16, BS, BS), f32),
             pltpu.VMEM((16, BS, BS), bf16),
-            pltpu.VMEM((12, PART, BS, BS), i16),
-            pltpu.VMEM((12, PART, BS), f32),
-            pltpu.VMEM((12, PART, BS, BS), i16),
-            pltpu.VMEM((12, PART, BS), f32),
+            pltpu.VMEM((6 * PARTS, PART, BS, BS), i16),
+            pltpu.VMEM((6 * PARTS, PART, BS), f32),
+            pltpu.VMEM((6 * PARTS, PART, BS, BS), i16),
+            pltpu.VMEM((6 * PARTS, PART, BS), f32),
             dma((2, 8)), dma((2, 8)), dma((2, 4, 6)), dma((2, 4, 6)),
             dma((2, 8)), dma((2, 8)), dma((2, 4, 4)), dma((2, 4, 4)), dma((5,)),
-            dma((2, 4, 4)), dma((12,)), dma((12,)), dma((12,)), dma((12,)), dma((2, 4)),
+            dma((2, 4, 2 * PARTS)), *[dma((6 * PARTS,))] * 4, dma((2, 2 * PARTS)),
         ],
         compiler_params=pltpu.CompilerParams(
-            collective_id=0, has_side_effects=True, vmem_limit_bytes=60 * 2**20
+            collective_id=0, has_side_effects=True, vmem_limit_bytes=44 * 2**20
         ),
         name="block_product",
-    )(a_blocks.reshape(64, BS, BS), b_blocks.reshape(32, BS, BS), c_pos, rows, cols)
+    )(*(pltpu.with_memory_space_constraint(x, pltpu.HBM) for x in (a_blocks.reshape(64, BS, BS), b_blocks.reshape(32, BS, BS), c_pos, rows, cols)))
     return out[None, None]
 
 

time: 111 us -> 108 us (0.973)
  Pallas kernels: 109 us -> 107 us
    pallas_call x1, Pallas kernels: 109 us -> 107 us  [per_device(): pl.pallas_call(kernel, out_shape=jax.ShapeDtypeStruct((16, BS, BS), bf16)...]
where the time goes in v2:
time: 108 us
  Pallas kernels  107 us (99%)
    pallas_call x1, Pallas kernels, per_device(): pl.pallas_call(kernel, out_shape=jax.ShapeDtypeStruct((16, BS, BS), bf16)...  107 us

profile of v2, /device:TPU:1, one launch (start us, length us, event | category | flops | bytes accessed | tf_op | source)
XLA Modules:
  0.0 108.2 jit_solution(18332314759929739795)
XLA Ops:
  0.0 107.4 %block_product.1 = bf16[16,128,128]{2,1,0:T(8,128)(2,1)S(1)} custom-call(bf16[64,128,128]{2,1,0:T(8,128)(2,1)} %bitcast.6, bf16[32,128,128]{2,1,0:T(8,128)(2,1)} %bitcast.7, s32[1,1,128]{2,1,0:T(1,128)} %c_ref.1, s32[4,4,16,32]{3,2,1,0:T(8,128)} %bitcast.8, s32[4,4,8,32]{3,2,1,0:T(8,128)} %bitcast.9), custom_call_target="tpu_custom_call" | custom-call | tf_op jit(solution)/shard_map/block_product/pallas_call | solution.py:412
  107.4 0.8 copy.7

commit v3 on v2

--- a/solution.py
+++ b/solution.py
@@ -86,6 +86,16 @@
     for step in (1, -1):
         greet(z_to(step))
         greet(x_to(step))
+    index_copies = [
+        pltpu.make_async_copy(c_ref, spots.at[0], c_sem.at[2]),
+        pltpu.make_async_copy(rows_ref.at[:, x], rows, c_sem.at[3]),
+        pltpu.make_async_copy(cols_ref.at[:, z], cols, c_sem.at[4]),
+    ]
+    for copy in index_copies:
+        copy.start()
+    for half in a_half:
+        for ref in half:
+            ref[ZERO] = jnp.zeros((BS, BS), jnp.bfloat16)
     pl.semaphore_wait(barrier, 18 + apart)
 
     waits = []
@@ -224,13 +234,13 @@
         copy.start()
         copy.wait()
 
-    def add_products(half, back, first, count, fresh=False):
+    def add_products(half, back, first, count, fresh=False, width=32):
         left_ref, right_ref = a_half[half][back], b_half[half]
         k = half * 8 + turned(z, -back)
 
         def some(n, _):
-            for s in range(32):
-                slot = first + n * 32 + s
+            for s in range(width):
+                slot = first + n * width + s
                 one, two = jobs[k, slot], jobs[k + 4, slot]
                 left = jnp.concatenate([left_ref[one >> 6], left_ref[two >> 6]], axis=1)
                 right = jnp.concatenate([right_ref[one & 63], right_ref[two & 63]], axis=0)
@@ -241,22 +251,12 @@
                     total[slot] += term
             return 0
 
-        lax.fori_loop(0, count // 32, some, 0)
+        lax.fori_loop(0, count // width, some, 0)
 
     hand_out_a(0)
     turn_a(0, 0)
     hand_out_b(0)
     send(c_ref, spots.at[1], c_sem.at[0], c_sem.at[1], twin)
-    index_copies = [
-        pltpu.make_async_copy(c_ref, spots.at[0], c_sem.at[2]),
-        pltpu.make_async_copy(rows_ref.at[:, x], rows, c_sem.at[3]),
-        pltpu.make_async_copy(cols_ref.at[:, z], cols, c_sem.at[4]),
-    ]
-    for copy in index_copies:
-        copy.start()
-    for half in a_half:
-        for ref in half:
-            ref[ZERO] = jnp.zeros((BS, BS), jnp.bfloat16)
     turn_a(0, 1)
     turn_b(0, 0)
     turn_a(0, 2)
@@ -319,13 +319,14 @@
         return turned(y, r) * 32
 
     def end_products(r):
-        add_products(1, 2, start_of(r), 32)
+        add_products(1, 2, start_of(r) + (1 - core) * 16, 16, width=16)
         for part in range(4):
             span = pl.ds(part * PART, PART)
             send(
                 total.at[pl.ds(start_of(r) + (1 - core) * 16 + part * PART, PART)], other.at[r, span],
                 twin_sem.at[0, r, part], twin_sem.at[1, r, part], twin,
             )
+        add_products(1, 2, start_of(r) + core * 16, 16, width=16)
 
     def meet(r, part):
         landed(other.at[r, pl.ds(part * PART, PART)], twin_sem.at[1, r, part])

time: 108 us -> 108 us (level)
  no operation moved by 1% of the time
where the time goes in v3:
time: 108 us
  Pallas kernels  107 us (99%)
    pallas_call x1, Pallas kernels, per_device(): pl.pallas_call(kernel, out_shape=jax.ShapeDtypeStruct((16, BS, BS), bf16)...  107 us

profile of v3, /device:TPU:1, one launch (start us, length us, event | category | flops | bytes accessed | tf_op | source)
XLA Modules:
  0.0 107.8 jit_solution(5111270151292908616)
XLA Ops:
  0.0 106.9 %block_product.1 = bf16[16,128,128]{2,1,0:T(8,128)(2,1)S(1)} custom-call(bf16[64,128,128]{2,1,0:T(8,128)(2,1)} %bitcast.6, bf16[32,128,128]{2,1,0:T(8,128)(2,1)} %bitcast.7, s32[1,1,128]{2,1,0:T(1,128)} %c_ref.1, s32[4,4,16,32]{3,2,1,0:T(8,128)} %bitcast.8, s32[4,4,8,32]{3,2,1,0:T(8,128)} %bitcast.9), custom_call_target="tpu_custom_call" | custom-call | tf_op jit(solution)/shard_map/block_product/pallas_call | solution.py:413
  107.0 0.8 copy.7

commit v4 on v3

--- a/solution.py
+++ b/solution.py
@@ -263,12 +263,12 @@
     pass_a(0, 0)
     pass_a(0, 1)
     turn_a(0, 3)
+    hand_out_a(1)
     pass_a(0, 2)
     turn_a(0, 4)
     turn_a(0, 5)
     turn_b(0, 1)
     turn_b(0, 2)
-    hand_out_a(1)
     hand_out_b(1)
     turn_b(0, 3)
     pass_a(0, 3)

time: 108 us -> 108 us (level)
  no operation moved by 1% of the time
where the time goes in v4:
time: 108 us
  Pallas kernels  107 us (99%)
    pallas_call x1, Pallas kernels, per_device(): pl.pallas_call(kernel, out_shape=jax.ShapeDtypeStruct((16, BS, BS), bf16)...  107 us

profile of v4, /device:TPU:1, one launch (start us, length us, event | category | flops | bytes accessed | tf_op | source)
XLA Modules:
  0.0 108.0 jit_solution(1849417816109895767)
XLA Ops:
  0.0 107.2 %block_product.1 = bf16[16,128,128]{2,1,0:T(8,128)(2,1)S(1)} custom-call(bf16[64,128,128]{2,1,0:T(8,128)(2,1)} %bitcast.6, bf16[32,128,128]{2,1,0:T(8,128)(2,1)} %bitcast.7, s32[1,1,128]{2,1,0:T(1,128)} %c_ref.1, s32[4,4,16,32]{3,2,1,0:T(8,128)} %bitcast.8, s32[4,4,8,32]{3,2,1,0:T(8,128)} %bitcast.9), custom_call_target="tpu_custom_call" | custom-call | tf_op jit(solution)/shard_map/block_product/pallas_call | solution.py:413
  107.2 0.8 copy.7

commit v5 on v3

--- a/solution.py
+++ b/solution.py
@@ -255,9 +255,9 @@
 
     hand_out_a(0)
     turn_a(0, 0)
-    hand_out_b(0)
     send(c_ref, spots.at[1], c_sem.at[0], c_sem.at[1], twin)
     turn_a(0, 1)
+    hand_out_b(0)
     turn_b(0, 0)
     turn_a(0, 2)
     pass_a(0, 0)

time: 108 us -> 108 us (level)
  no operation moved by 1% of the time
where the time goes in v5:
time: 108 us
  Pallas kernels  107 us (99%)
    pallas_call x1, Pallas kernels, per_device(): pl.pallas_call(kernel, out_shape=jax.ShapeDtypeStruct((16, BS, BS), bf16)...  107 us

profile of v5, /device:TPU:1, one launch (start us, length us, event | category | flops | bytes accessed | tf_op | source)
XLA Modules:
  0.0 107.9 jit_solution(14531073766201969555)
XLA Ops:
  0.0 107.1 %block_product.1 = bf16[16,128,128]{2,1,0:T(8,128)(2,1)S(1)} custom-call(bf16[64,128,128]{2,1,0:T(8,128)(2,1)} %bitcast.6, bf16[32,128,128]{2,1,0:T(8,128)(2,1)} %bitcast.7, s32[1,1,128]{2,1,0:T(1,128)} %c_ref.1, s32[4,4,16,32]{3,2,1,0:T(8,128)} %bitcast.8, s32[4,4,8,32]{3,2,1,0:T(8,128)} %bitcast.9), custom_call_target="tpu_custom_call" | custom-call | tf_op jit(solution)/shard_map/block_product/pallas_call | solution.py:413
  107.2 0.8 copy.7
